TPU v7x, 128 devices: a whole 4x4x4 slice. The times are simulated.
128 devices in a mesh: hid: 16 (over z, y), ffn: 8 (over x, core).
Axes of the slice: x: 4, y: 4, z: 4, core: 2. Of those that a mesh axis runs over, the one named last changes fastest.
Arguments:
- tokens: bfloat16 [128, 2, 16384], P('ffn', None, 'hid'), may hold values from -6 to 6
- norm_gain: bfloat16 [16384], P('hid'), may hold values from 0.099609375 to 1.8984375
- query_weight: bfloat16 [16384, 8192], P('hid', 'ffn'), may hold values from -0.046875 to 0.046875
- w_keyval: bfloat16 [16384, 1024], P('hid', 'ffn'), may hold values from -0.046875 to 0.046875
- w_out: bfloat16 [8192, 16384], P('ffn', 'hid'), may hold values from -0.25 to 0.25
- cache_keys: bfloat16 [128, 8192, 512], P(('hid', 'ffn')), may hold values from -1024 to 1024
- cache_values: bfloat16 [128, 8192, 512], P(('hid', 'ffn')), may hold values from -6 to 6
- lengths: int32 [128], replicated, may hold values from 2048 to 8192, as said below
Outputs:
- layer_out: bfloat16 [128, 2, 16384], P('ffn', None, 'hid')
- new_entries: bfloat16 [128, 2, 1024], P(('hid', 'ffn'))
Inputs may be any that keep to these rules, and one draw needn't show every extreme that they name: `lengths`: every prompt has from a quarter of 8192 to 8192 cached entries, and some prompt has exactly 8192.
All inputs are finite; a program needn't handle non-finite values.
Results may differ from a plain program's by a relative error of at most 0.02.
The roundings to bfloat16 on the way count: a program that leaves them out, or rounds other values in their place, can miss the bound.
Values may be sent and summed in bfloat16 or wider, within the bound.
A program may use at most 128 MiB of HBM per device.

v0:
```python
import functools

import jax
import jax.numpy as jnp
import numpy as np
from jax import lax
from jax.experimental import pallas as pl
from jax.experimental.pallas import tpu as pltpu
from jax.sharding import PartitionSpec as P

MESH = pl.DeviceIdType.MESH
F32 = jnp.float32
BF16 = jnp.bfloat16

HEADS = 64
KV_HEADS = 4
HD = 128
STEPS = 2
EPSILON = 1e-05
ROPE_BASE = 500000.0
SCALE = HD ** (-0.5) * 1.4426950408889634
MASKED = -1e30

NH = 16
NF = 8
NX = 4
NY = 4
LOW = 512
OWN = 32
PR = 16
CHUNK = 4096
CACHE_COPIES = 4
PAIRS = KV_HEADS // 2


def remote(src, dst, send_sem, recv_sem, device):
    return pltpu.make_async_remote_copy(
        src_ref=src,
        dst_ref=dst,
        send_sem=send_sem,
        recv_sem=recv_sem,
        device_id=device,
        device_id_type=MESH,
    )


def rotate(vectors, cosine, sine):
    return vectors * cosine + pltpu.roll(vectors, HD // 2, 1) * sine


def kernel(
    lengths_hbm, freq, tokens, gain, wq, wkv, wout, cache_k, cache_v,
    results,
    lengths, raw_v, tok_v, freq_v, gain_v, wq_v, wkv_v, wout_v, k_v, v_v,
    x_all, normed, ss_own, ss_recv, tot_all, part, relay_low, relay_high, left_low, left_high,
    right_low, right_high, mine, mine_recv,
    spread, msg, qkv, kx, vx, ne, scores, weighted, att_send, att_recv, att_f32, rows_all,
    opart, sib_recv, fin_send, fin_recv,
    local_sem, k_sem, v_sem,
    tok_ssem, tok_rsem, fwd_ssem, fwd_rsem, ss_ssem, ss_rsem, tot_ssem, tot_rsem,
    ring_ssem, ring_rsem, stage_ssem, stage_rsem, msg_ssem, msg_rsem, att_ssem, att_rsem, line_ssem, line_rsem,
    sib_ssem, sib_rsem, fin_ssem, fin_rsem,
):
    h = lax.axis_index("hid")
    f = lax.axis_index("ffn")
    z = lax.div(h, NY)
    y = lax.rem(h, NY)
    cx = lax.div(f, 2)
    core = lax.rem(f, 2)
    sib = f + 1 - 2 * core
    lmax = cache_k.shape[1]

    barrier = pltpu.get_barrier_semaphore()

    def greet_hid(k, carry):
        pl.semaphore_signal(
            barrier, inc=1, device_id=(lax.rem(h + k, NH), f), device_id_type=MESH
        )
        return carry

    def greet_ffn(k, carry):
        pl.semaphore_signal(
            barrier, inc=1, device_id=(h, lax.rem(f + k, NF)), device_id_type=MESH
        )
        return carry

    loads = []
    for i, (src, dst) in enumerate(
        [(tokens, raw_v), (gain, gain_v), (freq, freq_v), (wq, wq_v), (wkv, wkv_v), (lengths_hbm, lengths)]
    ):
        copy = pltpu.make_async_copy(src, dst, local_sem.at[i])
        copy.start()
        loads.append(copy)
    lax.fori_loop(1, NH, greet_hid, 0)
    lax.fori_loop(1, NF, greet_ffn, 0)

    span = lmax // CACHE_COPIES
    k_loads = []
    for i in range(CACHE_COPIES):
        copy = pltpu.make_async_copy(
            cache_k.at[0, pl.ds(i * span, span)], k_v.at[pl.ds(i * span, span)], k_sem.at[i]
        )
        copy.start()
        k_loads.append(copy)
    loads[0].wait()
    x_f32 = raw_v[...].astype(F32).reshape(tok_v.shape)
    x_own = x_f32.astype(BF16)
    tok_v[...] = x_own
    sums = jnp.sum(x_f32 * x_f32, axis=1, keepdims=True)
    row_id = lax.broadcasted_iota(jnp.int32, (OWN, HD), 0)
    lane_id = lax.broadcasted_iota(jnp.int32, (OWN, HD), 1)
    diagonal = row_id == lane_id
    own_sums = jnp.sum(jnp.where(diagonal, sums, 0.0), axis=0, keepdims=True)
    ss_own[...] = jnp.broadcast_to(own_sums, (8, HD))

    pl.semaphore_wait(barrier, NH + NF - 2)

    def block(index):
        return x_all.at[pl.ds(pl.multiple_of(index * OWN, OWN), OWN)]

    def ss_copy(k):
        return remote(
            ss_own, ss_recv.at[k - 1], ss_ssem.at[k - 1], ss_rsem.at[k - 1],
            (lax.rem(h + k, NH), f),
        )

    def ss_start(k, carry):
        ss_copy(k).start()
        return carry

    lax.fori_loop(1, NH, ss_start, 0)
    tok_copies = []
    for k in range(1, NX):
        peer = 2 * lax.rem(cx + k, NX) + core
        copy = remote(tok_v, block(f), tok_ssem.at[k - 1], tok_rsem.at[k - 1], (h, peer))
        copy.start()
        tok_copies.append(copy)
    fwd_copies = [remote(tok_v, block(f), fwd_ssem.at[0], fwd_rsem.at[0], (h, sib))]
    fwd_copies[0].start()
    x_all[pl.ds(pl.multiple_of(f * OWN, OWN), OWN), :] = x_own

    def ss_add(k, total):
        ss_copy(k).wait()
        return total + ss_recv[k - 1]

    total = lax.fori_loop(1, NH, ss_add, ss_own[...])
    tot_all[f] = total
    tot_copies = []
    for k in range(1, NF):
        copy = remote(
            tot_all.at[f], tot_all.at[f], tot_ssem.at[k - 1], tot_rsem.at[k - 1],
            (h, lax.rem(f + k, NF)),
        )
        copy.start()
        tot_copies.append(copy)
    for k in range(1, NX):
        tok_copies[k - 1].wait_recv()
        came = 2 * lax.rem(cx + NX - k, NX) + core
        copy = remote(block(came), block(came), fwd_ssem.at[k], fwd_rsem.at[k], (h, sib))
        copy.start()
        fwd_copies.append(copy)

    loads[5].wait()
    length = lengths[h * NF + f]
    step_of = lax.div(lax.broadcasted_iota(jnp.int32, (PR, HD), 0), 8)
    loads[2].wait()
    angles = (step_of + length).astype(F32) * freq_v[...]
    cosine = jnp.cos(angles)
    sine = jnp.sin(angles)
    sine = jnp.where(
        lax.broadcasted_iota(jnp.int32, (PR, HD), 1) < HD // 2, -sine, sine
    )

    for copy in tot_copies:
        copy.wait()
    loads[1].wait()
    width = x_all.shape[1]
    qcols = wq_v.shape[1]
    full = width * NH
    gain_row = gain_v[...].astype(F32).reshape(1, width)

    def project(parity):
        for x in range(NX):
            b = 2 * x + parity
            lane_sums = tot_all[b][0:1, :]
            row_sums = jnp.sum(jnp.where(diagonal, lane_sums, 0.0), axis=1, keepdims=True)
            inverse = lax.rsqrt(row_sums / full + EPSILON)
            normed[x * OWN : (x + 1) * OWN, :] = (
                block(b)[...].astype(F32) * inverse * gain_row
            ).astype(BF16)
        lhs = normed[...]
        for cols, weights in ((slice(0, qcols), wq_v), (slice(qcols, None), wkv_v)):
            product = jnp.dot(lhs, weights[...], preferred_element_type=F32)
            part[:, pl.ds(2 * parity, 2), :, cols] = product.reshape(NX, 2, PR, product.shape[1])

    loads[3].wait()
    loads[4].wait()
    project(core)
    for copy in fwd_copies:
        copy.wait()
    for copy in tok_copies:
        copy.wait_send()
    project(1 - core)

    half = PR // 2
    low, high_cols = pl.ds(0, LOW), pl.ds(LOW, part.shape[3] - LOW)

    def ring(side):
        pos = (y, z)[side]

        def device(q):
            return (z * NY + q, f) if side == 0 else (q * NY + y, f)

        def view(q, cols):
            if side == 0:
                return part.at[:, q, pl.ds(0, half), cols]
            return part.at[q, :, pl.ds(half, half), cols]

        return pos, device, view

    after = {}
    for side in range(2):
        pos, device, view = ring(side)
        nxt, prv, far = lax.rem(pos + 1, NY), lax.rem(pos + 3, NY), lax.rem(pos + 2, NY)
        plan = [
            (view(far, low), relay_low, nxt),
            (view(far, high_cols), relay_high, prv),
            (view(nxt, high_cols), left_high, nxt),
            (view(prv, low), right_low, prv),
        ]
        copies = [
            remote(
                src, dst.at[side], ring_ssem.at[side, i], ring_rsem.at[side, i], device(to)
            )
            for i, (src, dst, to) in enumerate(plan)
        ]
        after[side] = copies
    for first in (0, 2):
        for side in range(2):
            for copy in after[side][first : first + 2]:
                copy.start()
    v_loads = []
    for i in range(CACHE_COPIES):
        copy = pltpu.make_async_copy(
            cache_v.at[0, pl.ds(i * span, span)], v_v.at[pl.ds(i * span, span)], v_sem.at[i]
        )
        copy.start()
        v_loads.append(copy)
    wout_load = pltpu.make_async_copy(wout, wout_v, local_sem.at[6])
    wout_load.start()
    for side in range(2):
        pos, device, view = ring(side)
        nxt, prv = lax.rem(pos + 1, NY), lax.rem(pos + 3, NY)
        plan = [
            (view(nxt, low), relay_low, left_low, nxt),
            (view(prv, high_cols), relay_high, right_high, prv),
        ]
        for i, (own, relay, dst, to) in enumerate(plan):
            after[side][i].wait_recv()
            relay[side] = relay[side] + own[...]
            copy = remote(
                relay.at[side], dst.at[side],
                ring_ssem.at[side, 4 + i], ring_rsem.at[side, 4 + i], device(to),
            )
            copy.start()
            after[side].append(copy)
    stage_copies = {}
    for side in range(2):
        pos, device, view = ring(side)
        for copy in after[side][2:]:
            copy.wait_recv()
        mine[side, :, :, :LOW] = view(pos, low)[...] + left_low[side] + right_low[side]
        mine[side, :, :, LOW:] = view(pos, high_cols)[...] + left_high[side] + right_high[side]
        other, other_device, _ = ring(1 - side)
        stage_copies[side] = []
        for k in range(1, NY):
            peer = lax.rem(other + k, NY)
            copy = remote(
                mine.at[side, peer], mine_recv.at[side, k - 1],
                stage_ssem.at[side, k - 1], stage_rsem.at[side, k - 1], other_device(peer),
            )
            copy.start()
            stage_copies[side].append(copy)
    halves = []
    for side in range(2):
        other = ring(1 - side)[0]
        total = mine[side, other]
        for k in range(1, NY):
            stage_copies[side][k - 1].wait()
            total = total + mine_recv[side, k - 1]
        halves.append(total)
        for copy in after[side]:
            copy.wait_send()
    summed = jnp.concatenate(halves, axis=0)

    for j in range(8):
        spread[pl.ds(j, PR, stride=8), :] = summed[:, j * HD : (j + 1) * HD]
    msg[:, :PR, :] = spread[...].reshape(NF, PR, HD).astype(BF16)
    spread[...] = jnp.zeros_like(spread)
    spread[pl.ds(0, PR, stride=8), :] = summed[:, qcols:]
    msg[:, PR:, :] = spread[...].reshape(NF, PR, HD).astype(BF16)
    qkv[f] = msg[f]
    msg_copies = []
    for k in range(1, NF):
        peer = lax.rem(f + k, NF)
        copy = remote(
            msg.at[peer], qkv.at[f], msg_ssem.at[k - 1], msg_rsem.at[k - 1], (h, peer)
        )
        copy.start()
        msg_copies.append(copy)
    for copy in msg_copies:
        copy.wait()

    kx[...] = jnp.zeros_like(kx)
    vx[...] = jnp.zeros_like(vx)
    fresh_rows = []
    for i in range(2 * KV_HEADS):
        raw = qkv[i, PR:, :].astype(F32)
        cols = pl.ds((i % KV_HEADS) * HD, HD)
        if i < KV_HEADS:
            raw = rotate(raw, cosine, sine)
            kx[:PR, cols] = raw.astype(BF16)
        else:
            vx[:PR, cols] = raw.astype(BF16)
        fresh_rows.append(raw)

    rotated = [
        rotate(qkv[i, :PR, :].astype(F32), cosine, sine).astype(BF16) for i in range(NF)
    ]
    nothing = jnp.zeros((OWN, HD), BF16)
    queries = []
    for p in range(PAIRS):
        upper = jnp.concatenate(rotated[4 * p : 4 * p + 2], axis=0)
        lower = jnp.concatenate(rotated[4 * p + 2 : 4 * p + 4], axis=0)
        queries.append(
            jnp.concatenate(
                [
                    jnp.concatenate([upper, nothing], axis=1),
                    jnp.concatenate([nothing, lower], axis=1),
                ],
                axis=0,
            )
        )
    pair_rows, pair_cols = 2 * OWN, 2 * HD
    lane = lax.broadcasted_iota(jnp.int32, (pair_rows, HD), 1)
    step_row = lax.rem(lax.div(lax.broadcasted_iota(jnp.int32, (pair_rows, HD), 0), 8), 2)
    fresh_live = (lane == 0) | ((lane == 8) & (step_row == 1))
    nt = (((1,), (1,)), ((), ()))
    def attend(p):
        pair = pl.ds(p * pair_cols, pair_cols)
        rows_of = pl.ds(p * pair_rows, pair_rows)
        fresh = lax.dot_general(queries[p], kx[:, pair], nt, preferred_element_type=F32)
        fresh = jnp.where(fresh_live, fresh * SCALE, MASKED)

        def score_step(c, high):
            rows = pl.ds(pl.multiple_of(c * CHUNK, CHUNK), CHUNK)
            position = lax.broadcasted_iota(jnp.int32, (8, CHUNK), 1) + c * CHUNK
            cap = jnp.where(position < length, -MASKED, MASKED)
            cap = jnp.concatenate([cap] * (pair_rows // 8), axis=0)
            s = lax.dot_general(queries[p], k_v[rows, pair], nt, preferred_element_type=F32)
            s = jnp.minimum(s * SCALE, cap)
            scores[rows_of, rows] = s
            for t in range(CHUNK // HD):
                high = jnp.maximum(high, s[:, t * HD : (t + 1) * HD])
            return high

        high = lax.fori_loop(0, lmax // CHUNK, score_step, fresh)
        peak = jnp.broadcast_to(jnp.max(high, axis=1, keepdims=True), (pair_rows, HD))
        weights = jnp.exp2(fresh - peak).astype(BF16)
        weighted[p] = jnp.dot(weights, vx[:, pair], preferred_element_type=F32)

        def value_step(c, total):
            rows = pl.ds(pl.multiple_of(c * CHUNK, CHUNK), CHUNK)
            s = scores[rows_of, rows]
            pieces = []
            for t in range(CHUNK // HD):
                piece = jnp.exp2(s[:, t * HD : (t + 1) * HD] - peak).astype(BF16)
                total = total + piece.astype(F32)
                pieces.append(piece)
            weighted[p] += jnp.dot(
                jnp.concatenate(pieces, axis=1), v_v[rows, pair], preferred_element_type=F32
            )
            return total

        if p == 0:
            for copy in v_loads:
                copy.wait()
        total = lax.fori_loop(0, lmax // CHUNK, value_step, weights.astype(F32))
        weight_sum = jnp.sum(total, axis=1, keepdims=True)
        for i in range(2):
            rows = slice(i * OWN, (i + 1) * OWN)
            attended = weighted[p, rows, i * HD : (i + 1) * HD] / weight_sum[rows]
            attended = attended.astype(BF16)
            att_send[4 * p + 2 * i] = attended[:PR]
            att_send[4 * p + 2 * i + 1] = attended[PR:]

    odd = lax.rem(y + z, 2)
    slot = lax.rem(lax.div(y, 2) + lax.div(z, 2), 2)

    def send_attended(p):
        for m in range(4):
            peer = 4 * p + lax.rem(f + m, 4)
            landing = att_recv.at[odd, slot, f]

            @pl.when(peer == f)
            def _():
                pltpu.make_async_copy(
                    att_send.at[f], landing, att_rsem.at[odd, slot]
                ).start()

            for k in range(NY):
                chip = lax.rem(z + odd * k, NY) * NY + lax.rem(y + (1 - odd) * k, NY)
                copy = remote(
                    att_send.at[peer], landing, att_ssem.at[k], att_rsem.at[odd, slot],
                    (chip, peer),
                )
                if k == 0:
                    pl.when(peer != f)(copy.start)
                else:
                    copy.start()

    for copy in k_loads:
        copy.wait()
    for p in range(PAIRS):
        attend(p)
        send_attended(p)

    for i in range(2 * KV_HEADS):
        ne[0:1, i * HD : (i + 1) * HD] = fresh_rows[i][0:1]
        ne[1:2, i * HD : (i + 1) * HD] = fresh_rows[i][8:9]
    results[PR:, :, :] = ne[0:2, :].reshape(1, STEPS, ne.shape[1]).astype(BF16)

    line_copies = [[], []]
    for part_id in range(2):
        for side in range(2):
            whole = att_recv.at[side, part_id]
            pltpu.make_async_copy(whole, whole, att_rsem.at[side, part_id]).wait()
            pos = (z, y)[side]
            att_f32[...] = att_recv[side, part_id].astype(F32).reshape(NF * PR, HD)
            for j in range(8):
                rows_all[part_id, side, pos, :, j * HD : (j + 1) * HD] = att_f32[
                    pl.ds(j, PR, stride=8), :
                ].astype(BF16)
            mine_rows = rows_all.at[part_id, side, pos]
            for k in range(1, NY):
                q = lax.rem(pos + k, NY)
                device = (q * NY + y, f) if side == 0 else (z * NY + q, f)
                copy = remote(
                    mine_rows, mine_rows,
                    line_ssem.at[part_id, side, k - 1], line_rsem.at[part_id, side, k - 1],
                    device,
                )
                copy.start()
                line_copies[part_id].append(copy)
    wout_load.wait()

    def out_rows(index):
        return pl.ds(pl.multiple_of(index * OWN, OWN), OWN)

    sib_copies = [[], []]
    for part_id in range(2):
        for copy in line_copies[part_id]:
            copy.wait_recv()
        product = jnp.dot(
            rows_all[part_id].reshape(NH * PR // 2, wout_v.shape[0]),
            wout_v[...],
            preferred_element_type=F32,
        )
        for side in range(2):
            for q in range(NY):
                far = 2 * ((part_id + q // 2) % 2) + (q + side) % 2
                home = q * NY + far if side == 0 else far * NY + q
                first = (side * NY + q) * PR
                opart[home * PR : (home + 1) * PR, :] = product[first : first + PR]
        for e in range(2):
            x = 2 * lax.rem(1 + core + part_id, 2) + e
            copy = remote(
                opart.at[out_rows(2 * x + 1 - core)], sib_recv.at[part_id, e],
                sib_ssem.at[part_id, e], sib_rsem.at[part_id, e], (h, sib),
            )
            copy.start()
            sib_copies[part_id].append(copy)
    fin_copies = []
    for part_id in range(2):
        for copy in sib_copies[part_id]:
            copy.wait_recv()
        for e in range(2):
            x = 2 * lax.rem(core + part_id, 2) + e
            hop = lax.rem(x - cx + NX, NX)
            there = lax.rem(hop + NX - 1, NX)
            copy = remote(
                fin_send.at[part_id, e], fin_recv.at[there],
                fin_ssem.at[part_id, e], fin_rsem.at[there], (h, 2 * x + core),
            )
            fin_copies.append((hop, copy))

            @pl.when(hop != 0)
            def _():
                total = opart[out_rows(2 * x + core), :] + sib_recv[part_id, e]
                fin_send[part_id, e] = total.astype(BF16)
                copy.start()

    own_part = lax.rem(core + lax.div(cx, 2), 2)
    result = opart[out_rows(f), :] + sib_recv[own_part, lax.rem(cx, 2)]
    for k in range(1, NX):
        pltpu.make_async_copy(
            fin_recv.at[k - 1], fin_recv.at[k - 1], fin_rsem.at[k - 1]
        ).wait()
        result = result + fin_recv[k - 1].astype(F32)
    results[:PR, :, :] = result.reshape(PR, STEPS, result.shape[1]).astype(BF16)
    for hop, copy in fin_copies:
        pl.when(hop != 0)(copy.wait_send)
    for copies in sib_copies + line_copies:
        for copy in copies:
            copy.wait_send()
    for k in range(NY):
        sent = att_send.at[pl.ds(0, NF - 1)] if k == 0 else att_send
        pltpu.make_async_copy(sent, sent, att_ssem.at[k]).wait()


def hand_out(results, out, entries, sem):
    rows = out.shape[0]
    copies = [
        pltpu.make_async_copy(results.at[pl.ds(0, rows)], out, sem.at[0]),
        pltpu.make_async_copy(results.at[pl.ds(rows, 1)], entries, sem.at[1]),
    ]
    for copy in copies:
        copy.start()
    for copy in copies:
        copy.wait()


def body(tokens, norm_gain, query_weight, w_keyval, w_out, cache_keys, cache_values, lengths):
    width = tokens.shape[2]
    lmax = cache_keys.shape[1]
    qcols = query_weight.shape[1]
    kvcols = w_keyval.shape[1]
    halves = np.arange(HD // 2, dtype=np.float64) * (2.0 / HD)
    freq = (ROPE_BASE ** (-halves)).astype(np.float32)
    freq = jnp.asarray(np.tile(np.concatenate([freq, freq])[None, :], (PR, 1)))
    any_spec = pl.BlockSpec(memory_space=pl.ANY)
    hbm_spec = pl.BlockSpec(memory_space=pltpu.HBM)
    vmem_spec = pl.BlockSpec(memory_space=pltpu.VMEM)
    dma = pltpu.SemaphoreType.DMA
    rows = NH * PR
    results = pl.pallas_call(
        kernel,
        out_shape=pltpu.VMEM((PR + 1, STEPS, width), BF16),
        in_specs=[hbm_spec] * 9,
        out_specs=vmem_spec,
        scratch_shapes=[
            pltpu.SMEM(lengths.shape, jnp.int32),
            pltpu.VMEM(tokens.shape, BF16),
            pltpu.VMEM((OWN, width), BF16),
            pltpu.VMEM((PR, HD), F32),
            pltpu.VMEM((width,), BF16),
            pltpu.VMEM((width, qcols), BF16),
            pltpu.VMEM((width, kvcols), BF16),
            pltpu.VMEM((qcols, width), BF16),
            pltpu.VMEM((lmax, KV_HEADS * HD), BF16),
            pltpu.VMEM((lmax, KV_HEADS * HD), BF16),
            pltpu.VMEM((rows, width), BF16),
            pltpu.VMEM((rows // 2, width), BF16),
            pltpu.VMEM((8, HD), F32),
            pltpu.VMEM((NH - 1, 8, HD), F32),
            pltpu.VMEM((NF, 8, HD), F32),
            pltpu.VMEM((NY, NY, PR, qcols + kvcols), F32),
            pltpu.VMEM((2, NY, PR // 2, LOW), F32),
            pltpu.VMEM((2, NY, PR // 2, qcols + kvcols - LOW), F32),
            pltpu.VMEM((2, NY, PR // 2, LOW), F32),
            pltpu.VMEM((2, NY, PR // 2, qcols + kvcols - LOW), F32),
            pltpu.VMEM((2, NY, PR // 2, LOW), F32),
            pltpu.VMEM((2, NY, PR // 2, qcols + kvcols - LOW), F32),
            pltpu.VMEM((2, NY, PR // 2, qcols + kvcols), F32),
            pltpu.VMEM((2, NY - 1, PR // 2, qcols + kvcols), F32),
            pltpu.VMEM((NF * PR, HD), F32),
            pltpu.VMEM((NF, 2 * PR, HD), BF16),
            pltpu.VMEM((NF, 2 * PR, HD), BF16),
            pltpu.VMEM((HD, KV_HEADS * HD), BF16),
            pltpu.VMEM((HD, KV_HEADS * HD), BF16),
            pltpu.VMEM((8, 2 * KV_HEADS * HD), F32),
            pltpu.VMEM((KV_HEADS * OWN, lmax), F32),
            pltpu.VMEM((PAIRS, 2 * OWN, 2 * HD), F32),
            pltpu.VMEM((NF, PR, HD), BF16),
            pltpu.VMEM((2, 2, NF, PR, HD), BF16),
            pltpu.VMEM((NF * PR, HD), F32),
            pltpu.VMEM((2, 2, NY, PR, qcols), BF16),
            pltpu.VMEM((rows, width), F32),
            pltpu.VMEM((2, 2, OWN, width), F32),
            pltpu.VMEM((2, 2, OWN, width), BF16),
            pltpu.VMEM((NX - 1, OWN, width), BF16),
            dma((8,)),
            dma((CACHE_COPIES,)),
            dma((CACHE_COPIES,)),
            dma((NX - 1,)), dma((NX - 1,)),
            dma((NX,)), dma((NX,)),
            dma((NH - 1,)), dma((NH - 1,)),
            dma((NF - 1,)), dma((NF - 1,)),
            dma((2, 6)), dma((2, 6)),
            dma((2, NY - 1)), dma((2, NY - 1)),
            dma((NF - 1,)), dma((NF - 1,)),
            dma((NY,)), dma((2, 2)),
            dma((2, 2, NY - 1)), dma((2, 2, NY - 1)),
            dma((2, 2)), dma((2, 2)),
            dma((2, 2)), dma((NX - 1,)),
        ],
        compiler_params=pltpu.CompilerParams(
            collective_id=0, has_side_effects=True, vmem_limit_bytes=48 * 2**20
        ),
        name="decode_block",
    )(
        *[
            pltpu.with_memory_space_constraint(array, pltpu.HBM)
            for array in (
                lengths, freq, tokens, norm_gain, query_weight, w_keyval, w_out,
                cache_keys, cache_values,
            )
        ],
    )
    return pl.pallas_call(
        hand_out,
        out_shape=(
            jax.ShapeDtypeStruct(tokens.shape, BF16),
            jax.ShapeDtypeStruct((1, STEPS, 2 * KV_HEADS * HD), BF16),
        ),
        in_specs=[vmem_spec],
        out_specs=(any_spec, any_spec),
        scratch_shapes=[dma((2,))],
        name="hand_out",
    )(pltpu.with_memory_space_constraint(results, pltpu.VMEM))


def solution(mesh):
    in_specs = (
        P("ffn", None, "hid"),
        P("hid"),
        P("hid", "ffn"),
        P("hid", "ffn"),
        P("ffn", "hid"),
        P(("hid", "ffn"), None, None),
        P(("hid", "ffn"), None, None),
        P(),
    )
    out_specs = (P("ffn", None, "hid"), P(("hid", "ffn"), None, None))
    return jax.shard_map(body, mesh=mesh, in_specs=in_specs, out_specs=out_specs, check_vma=False)
```

profile of v0, /device:TPU:1, one launch (start us, length us, event | category | flops | bytes accessed | tf_op | source)
XLA Modules:
  0.0 59.7 jit_solution(16913130387540739826)
XLA Ops:
  0.6 58.4 %decode_block.1.results = bf16[17,2,1024]{2,1,0:T(2,128)(2,1)S(1)} custom-call(s32[128]{0:T(128)} %lengths_hbm.1, f32[16,128]{1,0:T(8,128)} %constant.2.clone.freq, bf16[16,2,1024]{2,1,0:T(2,128)(2,1)} %tokens.1, bf16[1024]{0:T(1024)(128)(2,1)} %gain.1, bf16[1024,1024]{1,0:T(8,128)(2,1)} %wq.1, bf16[1024,128]{1,0:T(8,128)(2,1)} %wkv.1, ...), custom_call_target="tpu_custom_call" | custom-call | tf_op jit(solution)/shard_map/decode_block/pallas_call | solution.py:546
  59.0 0.7 %hand_out.1 = (bf16[16,2,1024]{2,1,0:T(2,128)(2,1)}, bf16[1,2,1024]{2,1,0:T(2,128)(2,1)}) custom-call(bf16[17,2,1024]{2,1,0:T(2,128)(2,1)S(1)} %decode_block.1.results), custom_call_target="tpu_custom_call" | custom-call | tf_op jit(solution)/shard_map/hand_out/pallas_call | solution.py:620
where the time goes:
time: 59.8 us; the launch traced here: 59.7 us
  Pallas kernels  59 us (99%)
  between operations  0.64 us (1%)
    pallas_call x1, Pallas kernels, body(): pl.pallas_call(kernel, out_shape=pltpu.VMEM((PR + 1, STEPS, width), BF16)...  58.4 us

commit v1 on v0

--- a/solution.py
+++ b/solution.py
@@ -71,6 +71,8 @@
     lmax = cache_k.shape[1]
 
     barrier = pltpu.get_barrier_semaphore()
+    tokens_load = pltpu.make_async_copy(tokens, raw_v, local_sem.at[0])
+    tokens_load.start()
 
     def greet_hid(k, carry):
         pl.semaphore_signal(
@@ -84,16 +86,16 @@
         )
         return carry
 
+    lax.fori_loop(1, NF, greet_ffn, 0)
+    lax.fori_loop(1, NH, greet_hid, 0)
+
     loads = []
     for i, (src, dst) in enumerate(
-        [(tokens, raw_v), (gain, gain_v), (freq, freq_v), (wq, wq_v), (wkv, wkv_v), (lengths_hbm, lengths)]
+        [(gain, gain_v), (freq, freq_v), (wq, wq_v), (wkv, wkv_v), (lengths_hbm, lengths)]
     ):
-        copy = pltpu.make_async_copy(src, dst, local_sem.at[i])
+        copy = pltpu.make_async_copy(src, dst, local_sem.at[1 + i])
         copy.start()
         loads.append(copy)
-    lax.fori_loop(1, NH, greet_hid, 0)
-    lax.fori_loop(1, NF, greet_ffn, 0)
-
     span = lmax // CACHE_COPIES
     k_loads = []
     for i in range(CACHE_COPIES):
@@ -102,10 +104,27 @@
         )
         copy.start()
         k_loads.append(copy)
-    loads[0].wait()
+    wout_load = pltpu.make_async_copy(wout, wout_v, local_sem.at[6])
+    wout_load.start()
+
+    tokens_load.wait()
     x_f32 = raw_v[...].astype(F32).reshape(tok_v.shape)
     x_own = x_f32.astype(BF16)
     tok_v[...] = x_own
+    pl.semaphore_wait(barrier, NH + NF - 2)
+
+    def block(index):
+        return x_all.at[pl.ds(pl.multiple_of(index * OWN, OWN), OWN)]
+
+    tok_copies = []
+    for k in (1, 3, 2):
+        peer = 2 * lax.rem(cx + k, NX) + core
+        copy = remote(tok_v, block(f), tok_ssem.at[k - 1], tok_rsem.at[k - 1], (h, peer))
+        copy.start()
+        tok_copies.append((k, copy))
+    fwd_copies = [remote(tok_v, block(f), fwd_ssem.at[0], fwd_rsem.at[0], (h, sib))]
+    fwd_copies[0].start()
+
     sums = jnp.sum(x_f32 * x_f32, axis=1, keepdims=True)
     row_id = lax.broadcasted_iota(jnp.int32, (OWN, HD), 0)
     lane_id = lax.broadcasted_iota(jnp.int32, (OWN, HD), 1)
@@ -113,11 +132,6 @@
     own_sums = jnp.sum(jnp.where(diagonal, sums, 0.0), axis=0, keepdims=True)
     ss_own[...] = jnp.broadcast_to(own_sums, (8, HD))
 
-    pl.semaphore_wait(barrier, NH + NF - 2)
-
-    def block(index):
-        return x_all.at[pl.ds(pl.multiple_of(index * OWN, OWN), OWN)]
-
     def ss_copy(k):
         return remote(
             ss_own, ss_recv.at[k - 1], ss_ssem.at[k - 1], ss_rsem.at[k - 1],
@@ -129,18 +143,10 @@
         return carry
 
     lax.fori_loop(1, NH, ss_start, 0)
-    tok_copies = []
-    for k in range(1, NX):
-        peer = 2 * lax.rem(cx + k, NX) + core
-        copy = remote(tok_v, block(f), tok_ssem.at[k - 1], tok_rsem.at[k - 1], (h, peer))
-        copy.start()
-        tok_copies.append(copy)
-    fwd_copies = [remote(tok_v, block(f), fwd_ssem.at[0], fwd_rsem.at[0], (h, sib))]
-    fwd_copies[0].start()
     x_all[pl.ds(pl.multiple_of(f * OWN, OWN), OWN), :] = x_own
 
     def ss_add(k, total):
-        ss_copy(k).wait()
+        ss_copy(k).wait_recv()
         return total + ss_recv[k - 1]
 
     total = lax.fori_loop(1, NH, ss_add, ss_own[...])
@@ -153,17 +159,17 @@
         )
         copy.start()
         tot_copies.append(copy)
-    for k in range(1, NX):
-        tok_copies[k - 1].wait_recv()
+    for k, tok_copy in tok_copies:
+        tok_copy.wait_recv()
         came = 2 * lax.rem(cx + NX - k, NX) + core
         copy = remote(block(came), block(came), fwd_ssem.at[k], fwd_rsem.at[k], (h, sib))
         copy.start()
         fwd_copies.append(copy)
 
-    loads[5].wait()
+    loads[4].wait()
     length = lengths[h * NF + f]
     step_of = lax.div(lax.broadcasted_iota(jnp.int32, (PR, HD), 0), 8)
-    loads[2].wait()
+    loads[1].wait()
     angles = (step_of + length).astype(F32) * freq_v[...]
     cosine = jnp.cos(angles)
     sine = jnp.sin(angles)
@@ -171,9 +177,11 @@
         lax.broadcasted_iota(jnp.int32, (PR, HD), 1) < HD // 2, -sine, sine
     )
 
+    kx[...] = jnp.zeros_like(kx)
+    vx[...] = jnp.zeros_like(vx)
     for copy in tot_copies:
-        copy.wait()
-    loads[1].wait()
+        copy.wait_recv()
+    loads[0].wait()
     width = x_all.shape[1]
     qcols = wq_v.shape[1]
     full = width * NH
@@ -193,13 +201,11 @@
             product = jnp.dot(lhs, weights[...], preferred_element_type=F32)
             part[:, pl.ds(2 * parity, 2), :, cols] = product.reshape(NX, 2, PR, product.shape[1])
 
+    loads[2].wait()
     loads[3].wait()
-    loads[4].wait()
     project(core)
     for copy in fwd_copies:
-        copy.wait()
-    for copy in tok_copies:
-        copy.wait_send()
+        copy.wait_recv()
     project(1 - core)
 
     half = PR // 2
@@ -246,8 +252,14 @@
         )
         copy.start()
         v_loads.append(copy)
-    wout_load = pltpu.make_async_copy(wout, wout_v, local_sem.at[6])
-    wout_load.start()
+
+    def ss_sent(k, carry):
+        ss_copy(k).wait_send()
+        return carry
+
+    lax.fori_loop(1, NH, ss_sent, 0)
+    for copy in tot_copies + fwd_copies + [copy for _, copy in tok_copies]:
+        copy.wait_send()
     for side in range(2):
         pos, device, view = ring(side)
         nxt, prv = lax.rem(pos + 1, NY), lax.rem(pos + 3, NY)
@@ -286,11 +298,9 @@
         other = ring(1 - side)[0]
         total = mine[side, other]
         for k in range(1, NY):
-            stage_copies[side][k - 1].wait()
+            stage_copies[side][k - 1].wait_recv()
             total = total + mine_recv[side, k - 1]
         halves.append(total)
-        for copy in after[side]:
-            copy.wait_send()
     summed = jnp.concatenate(halves, axis=0)
 
     for j in range(8):
@@ -308,11 +318,12 @@
         )
         copy.start()
         msg_copies.append(copy)
+    for side in range(2):
+        for copy in after[side] + stage_copies[side]:
+            copy.wait_send()
     for copy in msg_copies:
-        copy.wait()
-
-    kx[...] = jnp.zeros_like(kx)
-    vx[...] = jnp.zeros_like(vx)
+        copy.wait_recv()
+
     fresh_rows = []
     for i in range(2 * KV_HEADS):
         raw = qkv[i, PR:, :].astype(F32)
@@ -453,6 +464,11 @@
                 copy.start()
                 line_copies[part_id].append(copy)
     wout_load.wait()
+    for copy in msg_copies:
+        copy.wait_send()
+    for k in range(NY):
+        sent = att_send.at[pl.ds(0, NF - 1)] if k == 0 else att_send
+        pltpu.make_async_copy(sent, sent, att_ssem.at[k]).wait()
 
     def out_rows(index):
         return pl.ds(pl.multiple_of(index * OWN, OWN), OWN)
@@ -500,6 +516,9 @@
                 fin_send[part_id, e] = total.astype(BF16)
                 copy.start()
 
+    for copies in sib_copies + line_copies:
+        for copy in copies:
+            copy.wait_send()
     own_part = lax.rem(core + lax.div(cx, 2), 2)
     result = opart[out_rows(f), :] + sib_recv[own_part, lax.rem(cx, 2)]
     for k in range(1, NX):
@@ -510,12 +529,6 @@
     results[:PR, :, :] = result.reshape(PR, STEPS, result.shape[1]).astype(BF16)
     for hop, copy in fin_copies:
         pl.when(hop != 0)(copy.wait_send)
-    for copies in sib_copies + line_copies:
-        for copy in copies:
-            copy.wait_send()
-    for k in range(NY):
-        sent = att_send.at[pl.ds(0, NF - 1)] if k == 0 else att_send
-        pltpu.make_async_copy(sent, sent, att_ssem.at[k]).wait()
 
 
 def hand_out(results, out, entries, sem):

time: 59.8 us -> 59.9 us (level)
  no operation moved by 1% of the time
where the time goes in v1:
time: 59.9 us; the launch traced here: 59.8 us
  Pallas kernels  59.1 us (99%)
  between operations  0.64 us (1%)
    pallas_call x1, Pallas kernels, body(): pl.pallas_call(kernel, out_shape=pltpu.VMEM((PR + 1, STEPS, width), BF16)...  58.5 us

profile of v1, /device:TPU:1, one launch (start us, length us, event | category | flops | bytes accessed | tf_op | source)
XLA Modules:
  0.0 59.8 jit_solution(15899300337843226392)
XLA Ops:
  0.6 58.5 %decode_block.1.results = bf16[17,2,1024]{2,1,0:T(2,128)(2,1)S(1)} custom-call(s32[128]{0:T(128)} %lengths_hbm.1, f32[16,128]{1,0:T(8,128)} %constant.2.clone.freq, bf16[16,2,1024]{2,1,0:T(2,128)(2,1)} %tokens.1, bf16[1024]{0:T(1024)(128)(2,1)} %gain.1, bf16[1024,1024]{1,0:T(8,128)(2,1)} %wq.1, bf16[1024,128]{1,0:T(8,128)(2,1)} %wkv.1, ...), custom_call_target="tpu_custom_call" | custom-call | tf_op jit(solution)/shard_map/decode_block/pallas_call | solution.py:559
  59.1 0.7 %hand_out.1 = (bf16[16,2,1024]{2,1,0:T(2,128)(2,1)}, bf16[1,2,1024]{2,1,0:T(2,128)(2,1)}) custom-call(bf16[17,2,1024]{2,1,0:T(2,128)(2,1)S(1)} %decode_block.1.results), custom_call_target="tpu_custom_call" | custom-call | tf_op jit(solution)/shard_map/hand_out/pallas_call | solution.py:633

commit v2 on v1

--- a/solution.py
+++ b/solution.py
@@ -25,7 +25,7 @@
 NF = 8
 NX = 4
 NY = 4
-LOW = 512
+GROUPS = (((0, 256), (256, 256)), ((512, 384), (896, 256)))
 OWN = 32
 PR = 16
 CHUNK = 4096
@@ -52,8 +52,7 @@
     lengths_hbm, freq, tokens, gain, wq, wkv, wout, cache_k, cache_v,
     results,
     lengths, raw_v, tok_v, freq_v, gain_v, wq_v, wkv_v, wout_v, k_v, v_v,
-    x_all, normed, ss_own, ss_recv, tot_all, part, relay_low, relay_high, left_low, left_high,
-    right_low, right_high, mine, mine_recv,
+    x_all, normed, ss_own, ss_recv, tot_all, part, relay, left, right, mine, mine_recv,
     spread, msg, qkv, kx, vx, ne, scores, weighted, att_send, att_recv, att_f32, rows_all,
     opart, sib_recv, fin_send, fin_recv,
     local_sem, k_sem, v_sem,
@@ -209,7 +208,6 @@
     project(1 - core)
 
     half = PR // 2
-    low, high_cols = pl.ds(0, LOW), pl.ds(LOW, part.shape[3] - LOW)
 
     def ring(side):
         pos = (y, z)[side]
@@ -224,27 +222,29 @@
 
         return pos, device, view
 
-    after = {}
-    for side in range(2):
-        pos, device, view = ring(side)
-        nxt, prv, far = lax.rem(pos + 1, NY), lax.rem(pos + 3, NY), lax.rem(pos + 2, NY)
-        plan = [
-            (view(far, low), relay_low, nxt),
-            (view(far, high_cols), relay_high, prv),
-            (view(nxt, high_cols), left_high, nxt),
-            (view(prv, low), right_low, prv),
-        ]
-        copies = [
-            remote(
-                src, dst.at[side], ring_ssem.at[side, i], ring_rsem.at[side, i], device(to)
-            )
-            for i, (src, dst, to) in enumerate(plan)
-        ]
-        after[side] = copies
+    moves = {}
+    for g, (low, high) in enumerate(GROUPS):
+        for side in range(2):
+            pos, device, view = ring(side)
+            nxt, prv, far = lax.rem(pos + 1, NY), lax.rem(pos + 3, NY), lax.rem(pos + 2, NY)
+            plan = [
+                (far, low, relay, nxt),
+                (far, high, relay, prv),
+                (nxt, high, left, nxt),
+                (prv, low, right, prv),
+            ]
+            moves[g, side] = [
+                remote(
+                    view(q, pl.ds(*cols)), dst.at[side, :, :, pl.ds(*cols)],
+                    ring_ssem.at[g, side, i], ring_rsem.at[g, side, i], device(to),
+                )
+                for i, (q, cols, dst, to) in enumerate(plan)
+            ]
     for first in (0, 2):
-        for side in range(2):
-            for copy in after[side][first : first + 2]:
-                copy.start()
+        for g in range(len(GROUPS)):
+            for side in range(2):
+                for copy in moves[g, side][first : first + 2]:
+                    copy.start()
     v_loads = []
     for i in range(CACHE_COPIES):
         copy = pltpu.make_async_copy(
@@ -260,48 +260,56 @@
     lax.fori_loop(1, NH, ss_sent, 0)
     for copy in tot_copies + fwd_copies + [copy for _, copy in tok_copies]:
         copy.wait_send()
-    for side in range(2):
-        pos, device, view = ring(side)
-        nxt, prv = lax.rem(pos + 1, NY), lax.rem(pos + 3, NY)
-        plan = [
-            (view(nxt, low), relay_low, left_low, nxt),
-            (view(prv, high_cols), relay_high, right_high, prv),
-        ]
-        for i, (own, relay, dst, to) in enumerate(plan):
-            after[side][i].wait_recv()
-            relay[side] = relay[side] + own[...]
-            copy = remote(
-                relay.at[side], dst.at[side],
-                ring_ssem.at[side, 4 + i], ring_rsem.at[side, 4 + i], device(to),
+    for g, (low, high) in enumerate(GROUPS):
+        for side in range(2):
+            pos, device, view = ring(side)
+            nxt, prv = lax.rem(pos + 1, NY), lax.rem(pos + 3, NY)
+            for i, (to, cols, dst) in enumerate(((nxt, low, left), (prv, high, right))):
+                cols = pl.ds(*cols)
+                moves[g, side][i].wait_recv()
+                passed = relay.at[side, :, :, cols]
+                passed[...] = passed[...] + view(to, cols)[...]
+                copy = remote(
+                    passed, dst.at[side, :, :, cols],
+                    ring_ssem.at[g, side, 4 + i], ring_rsem.at[g, side, 4 + i], device(to),
+                )
+                copy.start()
+                moves[g, side].append(copy)
+    stages = {}
+    for g, (low, high) in enumerate(GROUPS):
+        cols = pl.ds(low[0], low[1] + high[1])
+        for side in range(2):
+            pos, device, view = ring(side)
+            for copy in moves[g, side][2:]:
+                copy.wait_recv()
+            mine[side, :, :, cols] = (
+                view(pos, cols)[...] + left[side, :, :, cols] + right[side, :, :, cols]
             )
-            copy.start()
-            after[side].append(copy)
-    stage_copies = {}
-    for side in range(2):
-        pos, device, view = ring(side)
-        for copy in after[side][2:]:
-            copy.wait_recv()
-        mine[side, :, :, :LOW] = view(pos, low)[...] + left_low[side] + right_low[side]
-        mine[side, :, :, LOW:] = view(pos, high_cols)[...] + left_high[side] + right_high[side]
-        other, other_device, _ = ring(1 - side)
-        stage_copies[side] = []
-        for k in range(1, NY):
-            peer = lax.rem(other + k, NY)
-            copy = remote(
-                mine.at[side, peer], mine_recv.at[side, k - 1],
-                stage_ssem.at[side, k - 1], stage_rsem.at[side, k - 1], other_device(peer),
-            )
-            copy.start()
-            stage_copies[side].append(copy)
-    halves = []
-    for side in range(2):
-        other = ring(1 - side)[0]
-        total = mine[side, other]
-        for k in range(1, NY):
-            stage_copies[side][k - 1].wait_recv()
-            total = total + mine_recv[side, k - 1]
-        halves.append(total)
-    summed = jnp.concatenate(halves, axis=0)
+            other, other_device, _ = ring(1 - side)
+            stages[g, side] = []
+            for k in (1, 3, 2):
+                peer = lax.rem(other + k, NY)
+                copy = remote(
+                    mine.at[side, peer, :, cols], mine_recv.at[side, k - 1, :, cols],
+                    stage_ssem.at[g, side, k - 1], stage_rsem.at[g, side, k - 1],
+                    other_device(peer),
+                )
+                copy.start()
+                stages[g, side].append(copy)
+    groups = []
+    for g, (low, high) in enumerate(GROUPS):
+        cols = pl.ds(low[0], low[1] + high[1])
+        halves = []
+        for side in range(2):
+            other = ring(1 - side)[0]
+            total = mine[side, other, :, cols]
+            for copy in stages[g, side]:
+                copy.wait_recv()
+            for k in range(NY - 1):
+                total = total + mine_recv[side, k, :, cols]
+            halves.append(total)
+        groups.append(jnp.concatenate(halves, axis=0))
+    summed = jnp.concatenate(groups, axis=1)
 
     for j in range(8):
         spread[pl.ds(j, PR, stride=8), :] = summed[:, j * HD : (j + 1) * HD]
@@ -318,8 +326,8 @@
         )
         copy.start()
         msg_copies.append(copy)
-    for side in range(2):
-        for copy in after[side] + stage_copies[side]:
+    for key in moves:
+        for copy in moves[key] + stages[key]:
             copy.wait_send()
     for copy in msg_copies:
         copy.wait_recv()
@@ -578,12 +586,9 @@
             pltpu.VMEM((NH - 1, 8, HD), F32),
             pltpu.VMEM((NF, 8, HD), F32),
             pltpu.VMEM((NY, NY, PR, qcols + kvcols), F32),
-            pltpu.VMEM((2, NY, PR // 2, LOW), F32),
-            pltpu.VMEM((2, NY, PR // 2, qcols + kvcols - LOW), F32),
-            pltpu.VMEM((2, NY, PR // 2, LOW), F32),
-            pltpu.VMEM((2, NY, PR // 2, qcols + kvcols - LOW), F32),
-            pltpu.VMEM((2, NY, PR // 2, LOW), F32),
-            pltpu.VMEM((2, NY, PR // 2, qcols + kvcols - LOW), F32),
+            pltpu.VMEM((2, NY, PR // 2, qcols + kvcols), F32),
+            pltpu.VMEM((2, NY, PR // 2, qcols + kvcols), F32),
+            pltpu.VMEM((2, NY, PR // 2, qcols + kvcols), F32),
             pltpu.VMEM((2, NY, PR // 2, qcols + kvcols), F32),
             pltpu.VMEM((2, NY - 1, PR // 2, qcols + kvcols), F32),
             pltpu.VMEM((NF * PR, HD), F32),
@@ -609,8 +614,8 @@
             dma((NX,)), dma((NX,)),
             dma((NH - 1,)), dma((NH - 1,)),
             dma((NF - 1,)), dma((NF - 1,)),
-            dma((2, 6)), dma((2, 6)),
-            dma((2, NY - 1)), dma((2, NY - 1)),
+            dma((2, 2, 6)), dma((2, 2, 6)),
+            dma((2, 2, NY - 1)), dma((2, 2, NY - 1)),
             dma((NF - 1,)), dma((NF - 1,)),
             dma((NY,)), dma((2, 2)),
             dma((2, 2, NY - 1)), dma((2, 2, NY - 1)),

time: 59.9 us -> 59.6 us (level)
  no operation moved by 1% of the time
where the time goes in v2:
time: 59.6 us; the launch traced here: 59.5 us
  Pallas kernels  58.8 us (99%)
  between operations  0.64 us (1%)
    pallas_call x1, Pallas kernels, body(): pl.pallas_call(kernel, out_shape=pltpu.VMEM((PR + 1, STEPS, width), BF16)...  58.2 us

profile of v2, /device:TPU:1, one launch (start us, length us, event | category | flops | bytes accessed | tf_op | source)
XLA Modules:
  0.0 59.5 jit_solution(14011845191401930419)
XLA Ops:
  0.6 58.2 %decode_block.1.results = bf16[17,2,1024]{2,1,0:T(2,128)(2,1)S(1)} custom-call(s32[128]{0:T(128)} %lengths_hbm.1, f32[16,128]{1,0:T(8,128)} %constant.2.clone.freq, bf16[16,2,1024]{2,1,0:T(2,128)(2,1)} %tokens.1, bf16[1024]{0:T(1024)(128)(2,1)} %gain.1, bf16[1024,1024]{1,0:T(8,128)(2,1)} %wq.1, bf16[1024,128]{1,0:T(8,128)(2,1)} %wkv.1, ...), custom_call_target="tpu_custom_call" | custom-call | tf_op jit(solution)/shard_map/decode_block/pallas_call | solution.py:567
  58.8 0.7 %hand_out.1 = (bf16[16,2,1024]{2,1,0:T(2,128)(2,1)}, bf16[1,2,1024]{2,1,0:T(2,128)(2,1)}) custom-call(bf16[17,2,1024]{2,1,0:T(2,128)(2,1)S(1)} %decode_block.1.results), custom_call_target="tpu_custom_call" | custom-call | tf_op jit(solution)/shard_map/hand_out/pallas_call | solution.py:638

commit v3 on v2

--- a/solution.py
+++ b/solution.py
@@ -25,6 +25,7 @@
 NF = 8
 NX = 4
 NY = 4
+TURN = 512
 GROUPS = (((0, 256), (256, 256)), ((512, 384), (896, 256)))
 OWN = 32
 PR = 16
@@ -51,7 +52,7 @@
 def kernel(
     lengths_hbm, freq, tokens, gain, wq, wkv, wout, cache_k, cache_v,
     results,
-    lengths, raw_v, tok_v, freq_v, gain_v, wq_v, wkv_v, wout_v, k_v, v_v,
+    lengths, raw_v, tok_v, freq_v, gain_v, wq_v, wkv_v, wout_v, k_v, k_t, v_v,
     x_all, normed, ss_own, ss_recv, tot_all, part, relay, left, right, mine, mine_recv,
     spread, msg, qkv, kx, vx, ne, scores, weighted, att_send, att_recv, att_f32, rows_all,
     opart, sib_recv, fin_send, fin_recv,
@@ -105,6 +106,16 @@
         k_loads.append(copy)
     wout_load = pltpu.make_async_copy(wout, wout_v, local_sem.at[6])
     wout_load.start()
+
+    def turn_keys(quarter):
+        k_loads[quarter].wait()
+
+        def turn(i, carry):
+            rows = pl.ds(pl.multiple_of(quarter * span + i * TURN, TURN), TURN)
+            k_t[:, rows] = k_v[rows, :].T
+            return carry
+
+        lax.fori_loop(0, span // TURN, turn, 0)
 
     tokens_load.wait()
     x_f32 = raw_v[...].astype(F32).reshape(tok_v.shape)
@@ -260,6 +271,7 @@
     lax.fori_loop(1, NH, ss_sent, 0)
     for copy in tot_copies + fwd_copies + [copy for _, copy in tok_copies]:
         copy.wait_send()
+    turn_keys(0)
     for g, (low, high) in enumerate(GROUPS):
         for side in range(2):
             pos, device, view = ring(side)
@@ -275,6 +287,7 @@
                 )
                 copy.start()
                 moves[g, side].append(copy)
+    turn_keys(1)
     stages = {}
     for g, (low, high) in enumerate(GROUPS):
         cols = pl.ds(low[0], low[1] + high[1])
@@ -296,6 +309,7 @@
                 )
                 copy.start()
                 stages[g, side].append(copy)
+    turn_keys(2)
     groups = []
     for g, (low, high) in enumerate(GROUPS):
         cols = pl.ds(low[0], low[1] + high[1])
@@ -329,6 +343,7 @@
     for key in moves:
         for copy in moves[key] + stages[key]:
             copy.wait_send()
+    turn_keys(3)
     for copy in msg_copies:
         copy.wait_recv()
 
@@ -376,7 +391,7 @@
             position = lax.broadcasted_iota(jnp.int32, (8, CHUNK), 1) + c * CHUNK
             cap = jnp.where(position < length, -MASKED, MASKED)
             cap = jnp.concatenate([cap] * (pair_rows // 8), axis=0)
-            s = lax.dot_general(queries[p], k_v[rows, pair], nt, preferred_element_type=F32)
+            s = jnp.dot(queries[p], k_t[pair, rows], preferred_element_type=F32)
             s = jnp.minimum(s * SCALE, cap)
             scores[rows_of, rows] = s
             for t in range(CHUNK // HD):
@@ -438,8 +453,6 @@
                 else:
                     copy.start()
 
-    for copy in k_loads:
-        copy.wait()
     for p in range(PAIRS):
         attend(p)
         send_attended(p)
@@ -579,6 +592,7 @@
             pltpu.VMEM((width, kvcols), BF16),
             pltpu.VMEM((qcols, width), BF16),
             pltpu.VMEM((lmax, KV_HEADS * HD), BF16),
+            pltpu.VMEM((KV_HEADS * HD, lmax), BF16),
             pltpu.VMEM((lmax, KV_HEADS * HD), BF16),
             pltpu.VMEM((rows, width), BF16),
             pltpu.VMEM((rows // 2, width), BF16),

time: 59.6 us -> 58.5 us (0.982)
  Pallas kernels: 58.8 us -> 57.7 us
    pallas_call x1, Pallas kernels: 58.2 us -> 57.1 us  [body(): pl.pallas_call(kernel, out_shape=pltpu.VMEM((PR + 1, STEPS, width), BF16)...]
where the time goes in v3:
time: 58.5 us; the launch traced here: 58.4 us
  Pallas kernels  57.7 us (99%)
  between operations  0.64 us (1%)
    pallas_call x1, Pallas kernels, body(): pl.pallas_call(kernel, out_shape=pltpu.VMEM((PR + 1, STEPS, width), BF16)...  57.1 us

profile of v3, /device:TPU:1, one launch (start us, length us, event | category | flops | bytes accessed | tf_op | source)
XLA Modules:
  0.0 58.4 jit_solution(13932642585304059518)
XLA Ops:
  0.6 57.1 %decode_block.1.results = bf16[17,2,1024]{2,1,0:T(2,128)(2,1)S(1)} custom-call(s32[128]{0:T(128)} %lengths_hbm.1, f32[16,128]{1,0:T(8,128)} %constant.2.clone.freq, bf16[16,2,1024]{2,1,0:T(2,128)(2,1)} %tokens.1, bf16[1024]{0:T(1024)(128)(2,1)} %gain.1, bf16[1024,1024]{1,0:T(8,128)(2,1)} %wq.1, bf16[1024,128]{1,0:T(8,128)(2,1)} %wkv.1, ...), custom_call_target="tpu_custom_call" | custom-call | tf_op jit(solution)/shard_map/decode_block/pallas_call | solution.py:580
  57.7 0.7 %hand_out.1 = (bf16[16,2,1024]{2,1,0:T(2,128)(2,1)}, bf16[1,2,1024]{2,1,0:T(2,128)(2,1)}) custom-call(bf16[17,2,1024]{2,1,0:T(2,128)(2,1)S(1)} %decode_block.1.results), custom_call_target="tpu_custom_call" | custom-call | tf_op jit(solution)/shard_map/hand_out/pallas_call | solution.py:652

commit v4 on v1

--- a/solution.py
+++ b/solution.py
@@ -25,6 +25,7 @@
 NF = 8
 NX = 4
 NY = 4
+TURN = 512
 LOW = 512
 OWN = 32
 PR = 16
@@ -51,7 +52,7 @@
 def kernel(
     lengths_hbm, freq, tokens, gain, wq, wkv, wout, cache_k, cache_v,
     results,
-    lengths, raw_v, tok_v, freq_v, gain_v, wq_v, wkv_v, wout_v, k_v, v_v,
+    lengths, raw_v, tok_v, freq_v, gain_v, wq_v, wkv_v, wout_v, k_v, k_t, v_v,
     x_all, normed, ss_own, ss_recv, tot_all, part, relay_low, relay_high, left_low, left_high,
     right_low, right_high, mine, mine_recv,
     spread, msg, qkv, kx, vx, ne, scores, weighted, att_send, att_recv, att_f32, rows_all,
@@ -107,6 +108,16 @@
     wout_load = pltpu.make_async_copy(wout, wout_v, local_sem.at[6])
     wout_load.start()
 
+    def turn_keys(quarter):
+        k_loads[quarter].wait()
+
+        def turn(i, carry):
+            rows = pl.ds(pl.multiple_of(quarter * span + i * TURN, TURN), TURN)
+            k_t[:, rows] = k_v[rows, :].T
+            return carry
+
+        lax.fori_loop(0, span // TURN, turn, 0)
+
     tokens_load.wait()
     x_f32 = raw_v[...].astype(F32).reshape(tok_v.shape)
     x_own = x_f32.astype(BF16)
@@ -159,6 +170,7 @@
         )
         copy.start()
         tot_copies.append(copy)
+    turn_keys(0)
     for k, tok_copy in tok_copies:
         tok_copy.wait_recv()
         came = 2 * lax.rem(cx + NX - k, NX) + core
@@ -204,6 +216,7 @@
     loads[2].wait()
     loads[3].wait()
     project(core)
+    turn_keys(1)
     for copy in fwd_copies:
         copy.wait_recv()
     project(1 - core)
@@ -260,6 +273,7 @@
     lax.fori_loop(1, NH, ss_sent, 0)
     for copy in tot_copies + fwd_copies + [copy for _, copy in tok_copies]:
         copy.wait_send()
+    turn_keys(2)
     for side in range(2):
         pos, device, view = ring(side)
         nxt, prv = lax.rem(pos + 1, NY), lax.rem(pos + 3, NY)
@@ -276,6 +290,7 @@
             )
             copy.start()
             after[side].append(copy)
+    turn_keys(3)
     stage_copies = {}
     for side in range(2):
         pos, device, view = ring(side)
@@ -368,7 +383,7 @@
             position = lax.broadcasted_iota(jnp.int32, (8, CHUNK), 1) + c * CHUNK
             cap = jnp.where(position < length, -MASKED, MASKED)
             cap = jnp.concatenate([cap] * (pair_rows // 8), axis=0)
-            s = lax.dot_general(queries[p], k_v[rows, pair], nt, preferred_element_type=F32)
+            s = jnp.dot(queries[p], k_t[pair, rows], preferred_element_type=F32)
             s = jnp.minimum(s * SCALE, cap)
             scores[rows_of, rows] = s
             for t in range(CHUNK // HD):
@@ -430,8 +445,6 @@
                 else:
                     copy.start()
 
-    for copy in k_loads:
-        copy.wait()
     for p in range(PAIRS):
         attend(p)
         send_attended(p)
@@ -571,6 +584,7 @@
             pltpu.VMEM((width, kvcols), BF16),
             pltpu.VMEM((qcols, width), BF16),
             pltpu.VMEM((lmax, KV_HEADS * HD), BF16),
+            pltpu.VMEM((KV_HEADS * HD, lmax), BF16),
             pltpu.VMEM((lmax, KV_HEADS * HD), BF16),
             pltpu.VMEM((rows, width), BF16),
             pltpu.VMEM((rows // 2, width), BF16),

time: 59.9 us -> 59.7 us (level)
  no operation moved by 1% of the time
where the time goes in v4:
time: 59.7 us; the launch traced here: 59.5 us
  Pallas kernels  58.9 us (99%)
  between operations  0.64 us (1%)
    pallas_call x1, Pallas kernels, body(): pl.pallas_call(kernel, out_shape=pltpu.VMEM((PR + 1, STEPS, width), BF16)...  58.2 us

profile of v4, /device:TPU:1, one launch (start us, length us, event | category | flops | bytes accessed | tf_op | source)
XLA Modules:
  0.0 59.5 jit_solution(14130121254608070146)
XLA Ops:
  0.6 58.2 %decode_block.1.results = bf16[17,2,1024]{2,1,0:T(2,128)(2,1)S(1)} custom-call(s32[128]{0:T(128)} %lengths_hbm.1, f32[16,128]{1,0:T(8,128)} %constant.2.clone.freq, bf16[16,2,1024]{2,1,0:T(2,128)(2,1)} %tokens.1, bf16[1024]{0:T(1024)(128)(2,1)} %gain.1, bf16[1024,1024]{1,0:T(8,128)(2,1)} %wq.1, bf16[1024,128]{1,0:T(8,128)(2,1)} %wkv.1, ...), custom_call_target="tpu_custom_call" | custom-call | tf_op jit(solution)/shard_map/decode_block/pallas_call | solution.py:572
  58.9 0.7 %hand_out.1 = (bf16[16,2,1024]{2,1,0:T(2,128)(2,1)}, bf16[1,2,1024]{2,1,0:T(2,128)(2,1)}) custom-call(bf16[17,2,1024]{2,1,0:T(2,128)(2,1)S(1)} %decode_block.1.results), custom_call_target="tpu_custom_call" | custom-call | tf_op jit(solution)/shard_map/hand_out/pallas_call | solution.py:647

commit v5 on v3

--- a/solution.py
+++ b/solution.py
@@ -176,19 +176,6 @@
         copy.start()
         fwd_copies.append(copy)
 
-    loads[4].wait()
-    length = lengths[h * NF + f]
-    step_of = lax.div(lax.broadcasted_iota(jnp.int32, (PR, HD), 0), 8)
-    loads[1].wait()
-    angles = (step_of + length).astype(F32) * freq_v[...]
-    cosine = jnp.cos(angles)
-    sine = jnp.sin(angles)
-    sine = jnp.where(
-        lax.broadcasted_iota(jnp.int32, (PR, HD), 1) < HD // 2, -sine, sine
-    )
-
-    kx[...] = jnp.zeros_like(kx)
-    vx[...] = jnp.zeros_like(vx)
     for copy in tot_copies:
         copy.wait_recv()
     loads[0].wait()
@@ -214,6 +201,20 @@
     loads[2].wait()
     loads[3].wait()
     project(core)
+
+    loads[4].wait()
+    length = lengths[h * NF + f]
+    step_of = lax.div(lax.broadcasted_iota(jnp.int32, (PR, HD), 0), 8)
+    loads[1].wait()
+    angles = (step_of + length).astype(F32) * freq_v[...]
+    cosine = jnp.cos(angles)
+    sine = jnp.sin(angles)
+    sine = jnp.where(
+        lax.broadcasted_iota(jnp.int32, (PR, HD), 1) < HD // 2, -sine, sine
+    )
+    kx[...] = jnp.zeros_like(kx)
+    vx[...] = jnp.zeros_like(vx)
+
     for copy in fwd_copies:
         copy.wait_recv()
     project(1 - core)

time: 58.5 us -> 58.6 us (level)
  no operation moved by 1% of the time
where the time goes in v5:
time: 58.6 us; the launch traced here: 58.4 us
  Pallas kernels  57.8 us (99%)
  between operations  0.64 us (1%)
    pallas_call x1, Pallas kernels, body(): pl.pallas_call(kernel, out_shape=pltpu.VMEM((PR + 1, STEPS, width), BF16)...  57.1 us

profile of v5, /device:TPU:1, one launch (start us, length us, event | category | flops | bytes accessed | tf_op | source)
XLA Modules:
  0.0 58.4 jit_solution(4482622566677598260)
XLA Ops:
  0.6 57.1 %decode_block.1.results = bf16[17,2,1024]{2,1,0:T(2,128)(2,1)S(1)} custom-call(s32[128]{0:T(128)} %lengths_hbm.1, f32[16,128]{1,0:T(8,128)} %constant.2.clone.freq, bf16[16,2,1024]{2,1,0:T(2,128)(2,1)} %tokens.1, bf16[1024]{0:T(1024)(128)(2,1)} %gain.1, bf16[1024,1024]{1,0:T(8,128)(2,1)} %wq.1, bf16[1024,128]{1,0:T(8,128)(2,1)} %wkv.1, ...), custom_call_target="tpu_custom_call" | custom-call | tf_op jit(solution)/shard_map/decode_block/pallas_call | solution.py:581
  57.8 0.7 %hand_out.1 = (bf16[16,2,1024]{2,1,0:T(2,128)(2,1)}, bf16[1,2,1024]{2,1,0:T(2,128)(2,1)}) custom-call(bf16[17,2,1024]{2,1,0:T(2,128)(2,1)S(1)} %decode_block.1.results), custom_call_target="tpu_custom_call" | custom-call | tf_op jit(solution)/shard_map/hand_out/pallas_call | solution.py:653
